TPU v7x, 32 devices: a whole 2x2x4 slice. The times are simulated.
32 devices in a mesh: dp: 16 (over z, x, core), tensor: 2 (over y).
Axes of the slice: x: 2, y: 2, z: 4, core: 2. Of those that a mesh axis runs over, the one named last changes fastest.
Arguments:
- tokens: bfloat16 [16384, 1024], P(('dp', 'tensor')), may hold values from -6 to 6
- gains: float32 [2, 1024], replicated, may hold values from 0.5 to 1.5
- shifts: float32 [4, 1024], replicated, may hold values from -1.8 to 1.8
- w_qkv: bfloat16 [1024, 3, 1024], P('dp', None, 'tensor'), may hold values from -0.1875 to 0.1875
- bias_qv: float32 [2, 1024], P(None, 'tensor'), may hold values from -1.8 to 1.8
- w_out: bfloat16 [1024, 1024], P('tensor', 'dp'), may hold values from -1 to 1
- w_in: bfloat16 [1024, 4096], P('dp', 'tensor'), may hold values from -0.1875 to 0.1875
- bias_in: float32 [4096], P('tensor'), may hold values from -1.8 to 1.8
- w_down: bfloat16 [4096, 1024], P('tensor', 'dp'), may hold values from -0.09375 to 0.09375
- segments: int32 [16, 1024], P('dp'), may hold values from 0 to 2, never falling along the last dimension, each value on 1 to 512 neighbouring positions
- grad_output: bfloat16 [16384, 1024], P(('dp', 'tensor')), may hold values from -6 to 6
Outputs:
- output: bfloat16 [16384, 1024], P(('dp', 'tensor'))
- input_grad: bfloat16 [16384, 1024], P(('dp', 'tensor'))
- gains_grad: float32 [2, 1024], P(None, ('dp', 'tensor'))
- shifts_grad: float32 [4, 1024], P(None, ('dp', 'tensor'))
- w_qkv_grad: float32 [1024, 3, 1024], P('dp', None, 'tensor')
- bias_qv_grad: float32 [2, 1024], P(None, ('tensor', 'dp'))
- w_out_grad: float32 [1024, 1024], P('tensor', 'dp')
- w_in_grad: float32 [1024, 4096], P('dp', 'tensor')
- bias_in_grad: float32 [4096], P(('tensor', 'dp'))
- w_down_grad: float32 [4096, 1024], P('tensor', 'dp')
Inputs may be any that keep to these rules, and one draw needn't show every extreme that they name: `segments`: along each sequence the numbers never fall; each document spans 1 to 512 tokens.
All inputs are finite; a program needn't handle non-finite values.
Results may differ from a plain program's by a relative error of at most 0.02.
Values may be sent and summed in bfloat16 or wider, within the bound.
A program may use at most 192 MiB of HBM per device.

v0:
```python
import math

import jax
import jax.numpy as jnp
from jax import lax
from jax.sharding import PartitionSpec as P

HEAD_DIM = 64


EPS = 1e-05
MASKED = -1000000000.0
GELU_C = 0.7978845608028654


def layer_norm(value, gain, shift):
    centre = value - jnp.mean(value, axis=-1, keepdims=True)
    spread = jnp.mean(centre * centre, axis=-1, keepdims=True)
    return centre * lax.rsqrt(spread + EPS) * gain + shift


def gelu_tanh(value):
    return 0.5 * value * (1.0 + jnp.tanh(GELU_C * (value + 0.044715 * value * value * value)))


def collect(first, second):
    return (
        lax.all_gather(first, "dp", axis=0, tiled=True),
        lax.all_gather(second, "dp", axis=1, tiled=True),
    )


def spread_rows(rows):
    return lax.all_gather(rows, "tensor", axis=0, tiled=True)


def project_sum(values, weight):
    part = lax.dynamic_slice_in_dim(
        values,
        jnp.int32(0),
        values.shape[0] // lax.axis_size("tensor") * lax.axis_size("tensor"),
        0,
    )
    return lax.psum_scatter(
        jnp.dot(part, weight, preferred_element_type=jnp.float32).astype(jnp.bfloat16),
        "tensor",
        scatter_dimension=0,
        tiled=True,
    ).astype(jnp.float32)


def output_projection(values, weight):
    return project_sum(values, weight)


def grad_sum(values, weight):
    part = lax.dynamic_slice_in_dim(
        values,
        jnp.int32(0),
        values.shape[0] // lax.axis_size("tensor") * lax.axis_size("tensor"),
        0,
    )
    return lax.psum_scatter(
        lax.dot_general(
            part, weight, (((1,), (1,)), ((), ())), preferred_element_type=jnp.float32
        ).astype(jnp.bfloat16),
        "tensor",
        scatter_dimension=0,
        tiled=True,
    ).astype(jnp.float32)


def input_grad_projection(values, weight):
    return grad_sum(values, weight)


def masks_for(seg, start, end):
    positions = jnp.arange(end, dtype=jnp.int32)
    same = seg[start:end, None] == seg[None, :end]
    causal = positions[start:end, None] >= positions[None, :end]
    return same & causal


def attention_forward(query, key, value, segments, scale):
    length = query.shape[1]
    block = min(512, length)
    blocks = length // block

    def one_seq(items):
        q_seq, k_seq, v_seq, seg = items
        outs = []
        sums = []
        for index in range(blocks):
            start = index * block
            end = start + block
            allowed = masks_for(seg, start, end)
            scores = (
                jnp.einsum(
                    "qhd,khd->hqk",
                    q_seq[start:end],
                    k_seq[:end],
                    preferred_element_type=jnp.float32,
                )
                * scale
            )
            scores = jnp.where(allowed[None], scores, MASKED)
            top = jnp.max(scores, axis=-1, keepdims=True)
            expo = jnp.exp(scores - top)
            total = jnp.sum(expo, axis=-1, keepdims=True)
            probs = (expo / total).astype(jnp.bfloat16)
            outs.append(
                jnp.einsum("hqk,khd->qhd", probs, v_seq[:end], preferred_element_type=jnp.float32)
            )
            sums.append((top + jnp.log(total))[..., 0])
        return (jnp.concatenate(outs, 0), jnp.concatenate(sums, 1))

    return lax.map(one_seq, (query, key, value, segments))


def attention_backward(query, key, value, segments, logsum, grad_att, scale):
    length = query.shape[1]
    block = min(512, length)
    blocks = length // block

    def one_seq(items):
        q_seq, k_seq, v_seq, seg, lse, do_seq = items
        dq_parts = []
        key_grad = jnp.zeros(k_seq.shape, jnp.float32)
        value_grad = jnp.zeros(v_seq.shape, jnp.float32)
        for index in range(blocks):
            start = index * block
            end = start + block
            allowed = masks_for(seg, start, end)
            q_rows = q_seq[start:end]
            do_rows = do_seq[start:end]
            scores = (
                jnp.einsum("qhd,khd->hqk", q_rows, k_seq[:end], preferred_element_type=jnp.float32)
                * scale
            )
            scores = jnp.where(allowed[None], scores, MASKED)
            probs = jnp.exp(scores - lse[:, start:end, None])
            probs_low = probs.astype(jnp.bfloat16)
            dprobs = jnp.einsum(
                "qhd,khd->hqk", do_rows, v_seq[:end], preferred_element_type=jnp.float32
            )
            inner = jnp.sum(dprobs * probs, axis=-1, keepdims=True)
            dscores = (probs * (dprobs - inner)).astype(jnp.bfloat16)
            dq_parts.append(
                jnp.einsum("hqk,khd->qhd", dscores, k_seq[:end], preferred_element_type=jnp.float32)
                * scale
            )
            key_grad = key_grad.at[:end].add(
                jnp.einsum("hqk,qhd->khd", dscores, q_rows, preferred_element_type=jnp.float32)
                * scale
            )
            value_grad = value_grad.at[:end].add(
                jnp.einsum("hqk,qhd->khd", probs_low, do_rows, preferred_element_type=jnp.float32)
            )
        return (jnp.concatenate(dq_parts, 0), key_grad, value_grad)

    return lax.map(one_seq, (query, key, value, segments, logsum, grad_att))


def per_device(
    tokens, gains, shifts, w_qkv, bias_qv, w_out, w_in, bias_in, w_down, segments, grad_output
):
    seqs, length = segments.shape
    scale = 1.0 / math.sqrt(HEAD_DIM)
    qkv_full, out_full = collect(w_qkv, w_out)
    in_full, down_full = collect(w_in, w_down)
    model = tokens.shape[1]
    local_width = qkv_full.shape[2]
    heads = local_width // HEAD_DIM
    rows_in = tokens.astype(jnp.float32)
    normed_one = layer_norm(rows_in, gains[0], shifts[0])
    full_a = spread_rows(normed_one.astype(jnp.bfloat16))
    total = full_a.shape[0]
    mixed = jnp.dot(
        full_a, qkv_full.reshape(model, 3 * local_width), preferred_element_type=jnp.float32
    )
    mixed = mixed.reshape(total, 3, local_width)
    mixed = mixed + jnp.stack([bias_qv[0], jnp.zeros_like(bias_qv[0]), bias_qv[1]])[None]
    shaped = mixed.astype(jnp.bfloat16).reshape(seqs, length, 3, heads, HEAD_DIM)
    query = shaped[:, :, 0]
    key = shaped[:, :, 1]
    value = shaped[:, :, 2]
    attended, logsum = attention_forward(query, key, value, segments, scale)
    attended_low = attended.reshape(total, local_width).astype(jnp.bfloat16)
    middle = rows_in + output_projection(attended_low, out_full) + shifts[1]
    normed_two = layer_norm(middle, gains[1], shifts[2])
    full_m = spread_rows(normed_two.astype(jnp.bfloat16))
    hidden_pre = jnp.dot(full_m, in_full, preferred_element_type=jnp.float32) + bias_in
    hidden_low = gelu_tanh(hidden_pre).astype(jnp.bfloat16)
    result = middle + output_projection(hidden_low, down_full) + shifts[3]
    output = result.astype(jnp.bfloat16)
    grad_rows = grad_output.astype(jnp.float32)
    full_dy = spread_rows(grad_output)
    down_grad = lax.dot_general(
        hidden_low, full_dy, (((0,), (0,)), ((), ())), preferred_element_type=jnp.float32
    )
    hidden_grad = lax.dot_general(
        full_dy, down_full, (((1,), (1,)), ((), ())), preferred_element_type=jnp.float32
    )
    gelu_out, gelu_back = jax.vjp(gelu_tanh, hidden_pre)
    pre_grad = gelu_back(hidden_grad)[0].astype(jnp.bfloat16)
    bias_in_part = jnp.sum(pre_grad, axis=0, dtype=jnp.float32)
    in_grad = lax.dot_general(
        full_m, pre_grad, (((0,), (0,)), ((), ())), preferred_element_type=jnp.float32
    )
    ff_in, ff_down, ff_bias = (
        lax.psum_scatter(
            in_grad.astype(jnp.bfloat16), "dp", scatter_dimension=0, tiled=True
        ).astype(jnp.float32),
        lax.psum_scatter(
            down_grad.astype(jnp.bfloat16), "dp", scatter_dimension=1, tiled=True
        ).astype(jnp.float32),
        lax.psum_scatter(
            bias_in_part.astype(jnp.bfloat16), "dp", scatter_dimension=0, tiled=True
        ).astype(jnp.float32),
    )
    normed_two_grad = input_grad_projection(pre_grad, in_full)
    norm_two_out, norm_two_back = jax.vjp(layer_norm, middle, gains[1], shifts[2])
    middle_part, gain_two_grad, shift_two_grad = norm_two_back(normed_two_grad)
    middle_grad = grad_rows + middle_part
    branch_low = middle_grad.astype(jnp.bfloat16)
    full_branch = spread_rows(branch_low)
    out_grad = lax.dot_general(
        attended_low, full_branch, (((0,), (0,)), ((), ())), preferred_element_type=jnp.float32
    )
    attended_grad = lax.dot_general(
        full_branch, out_full, (((1,), (1,)), ((), ())), preferred_element_type=jnp.float32
    )
    attended_grad_low = attended_grad.astype(jnp.bfloat16).reshape(seqs, length, heads, HEAD_DIM)
    query_grad, key_grad, value_grad = attention_backward(
        query, key, value, segments, logsum, attended_grad_low, scale
    )
    mixed_grad = jnp.stack([query_grad, key_grad, value_grad], 2).astype(jnp.bfloat16)
    mixed_flat = mixed_grad.reshape(total, 3 * local_width)
    qkv_grad = lax.dot_general(
        full_a, mixed_flat, (((0,), (0,)), ((), ())), preferred_element_type=jnp.float32
    )
    qkv_grad = qkv_grad.reshape(model, 3, local_width)
    mixed_three = mixed_grad.reshape(total, 3, local_width)
    bias_qv_part = jnp.stack(
        [
            jnp.sum(mixed_three[:, 0], axis=0, dtype=jnp.float32),
            jnp.sum(mixed_three[:, 2], axis=0, dtype=jnp.float32),
        ]
    )
    att_qkv, att_out, att_bias = (
        lax.psum_scatter(
            qkv_grad.astype(jnp.bfloat16), "dp", scatter_dimension=0, tiled=True
        ).astype(jnp.float32),
        lax.psum_scatter(
            out_grad.astype(jnp.bfloat16), "dp", scatter_dimension=1, tiled=True
        ).astype(jnp.float32),
        lax.psum_scatter(
            bias_qv_part.astype(jnp.bfloat16), "dp", scatter_dimension=1, tiled=True
        ).astype(jnp.float32),
    )
    normed_one_grad = input_grad_projection(mixed_flat, qkv_full.reshape(model, 3 * local_width))
    norm_one_out, norm_one_back = jax.vjp(layer_norm, rows_in, gains[0], shifts[0])
    input_part, gain_one_grad, shift_one_grad = norm_one_back(normed_one_grad)
    input_grad = (middle_grad + input_part).astype(jnp.bfloat16)
    gain_parts = jnp.stack([gain_one_grad, gain_two_grad])
    shift_parts = jnp.stack(
        [
            shift_one_grad,
            jnp.sum(branch_low, axis=0, dtype=jnp.float32),
            shift_two_grad,
            jnp.sum(grad_rows, axis=0),
        ]
    )
    gains_grad, shifts_grad = (
        lax.psum_scatter(gain_parts, ("dp", "tensor"), scatter_dimension=1, tiled=True),
        lax.psum_scatter(shift_parts, ("dp", "tensor"), scatter_dimension=1, tiled=True),
    )
    return (
        output,
        input_grad,
        gains_grad,
        shifts_grad,
        att_qkv,
        att_bias,
        att_out,
        ff_in,
        ff_bias,
        ff_down,
    )


def solution(mesh):
    placed = (
        P(("dp", "tensor"), None),
        P(),
        P(),
        P("dp", None, "tensor"),
        P(None, "tensor"),
        P("tensor", "dp"),
        P("dp", "tensor"),
        P("tensor"),
        P("tensor", "dp"),
        P("dp", None),
        P(("dp", "tensor"), None),
    )
    return jax.shard_map(
        per_device,
        mesh=mesh,
        in_specs=placed,
        out_specs=(
            P(("dp", "tensor"), None),
            P(("dp", "tensor"), None),
            P(None, ("dp", "tensor")),
            P(None, ("dp", "tensor")),
            P("dp", None, "tensor"),
            P(None, ("tensor", "dp")),
            P("tensor", "dp"),
            P("dp", "tensor"),
            P(("tensor", "dp")),
            P("tensor", "dp"),
        ),
        check_vma=False,
    )
```

profile of v0, /device:TPU:0, one launch (start us, length us, event | category | flops | bytes accessed | tf_op | source)
XLA Modules:
  0.0 1178.8 jit_solution(10564277248462500966)
XLA Ops:
  17.8 40.4 %all-gather.11.cloned.1.call-done = bf16[1024,3,512]{2,0,1:T(8,128)(2,1)} async-done(((bf16[64,3,512]{2,0,1:T(8,128)(2,1)}), bf16[1024,3,512]{2,0,1:T(8,128)(2,1)}) %all-gather.11.cloned.1.call-update) | async-done | bytes 3145744 | tf_op jit(solution)/shard_map/all_gather | solution.py:28
  62.8 29.4 %all-gather.9.cloned.1.call-done = bf16[1024,1024]{1,0:T(8,128)(2,1)} async-done(((bf16[512,1024]{1,0:T(8,128)(2,1)}), bf16[1024,1024]{1,0:T(8,128)(2,1)}) %all-gather.9.cloned.1.call-update) | async-done | bytes 2097168 | tf_op jit(solution)/shard_map/all_gather | solution.py:34
  117.6 14.7 %all-gather.13.cloned.1.call-done = bf16[512,1024]{0,1:T(8,128)(2,1)} async-done(((bf16[512,64]{0,1:T(8,128)(2,1)}), bf16[512,1024]{0,1:T(8,128)(2,1)}) %all-gather.13.cloned.1.call-update) | async-done | bytes 1048592 | tf_op jit(solution)/shard_map/all_gather | solution.py:29
  136.9 30.3 %reduce-scatter.18.cloned.1.call-done = bf16[512,1024]{1,0:T(8,128)(2,1)} async-done(((bf16[1024,1024]{1,0:T(8,128)(2,1)}), bf16[512,1024]{1,0:T(8,128)(2,1)}) %reduce-scatter.18.cloned.1.call-update) | async-done | bytes 1048592 | tf_op jit(solution)/shard_map/reduce_scatter | solution.py:44
  173.9 46.1 %all-gather.17.cloned.1.call-done = bf16[1024,2048]{1,0:T(8,128)(2,1)} async-done(((bf16[64,2048]{1,0:T(8,128)(2,1)}), bf16[1024,2048]{1,0:T(8,128)(2,1)}) %all-gather.17.cloned.1.call-update) | async-done | bytes 4194320 | tf_op jit(solution)/shard_map/all_gather | solution.py:28
  220.1 33.7 %all-gather.15.cloned.1.call-done = bf16[1024,1024]{1,0:T(8,128)(2,1)} async-done(((bf16[512,1024]{1,0:T(8,128)(2,1)}), bf16[1024,1024]{1,0:T(8,128)(2,1)}) %all-gather.15.cloned.1.call-update) | async-done | bytes 2097168 | tf_op jit(solution)/shard_map/all_gather | solution.py:34
  253.8 10.9 fusion.79
  264.6 23.9 %all-gather.21.cloned.1.call-done = bf16[1024,1024]{1,0:T(8,128)(2,1)} async-done(((bf16[512,1024]{1,0:T(8,128)(2,1)}), bf16[1024,1024]{1,0:T(8,128)(2,1)}) %all-gather.21.cloned.1.call-update) | async-done | bytes 2097168 | tf_op jit(solution)/shard_map/all_gather | solution.py:34
  288.5 53.0 %all-gather.19.cloned.1.call-done = bf16[2048,1024]{0,1:T(8,128)(2,1)} async-done(((bf16[2048,64]{0,1:T(8,128)(2,1)}), bf16[2048,1024]{0,1:T(8,128)(2,1)}) %all-gather.19.cloned.1.call-update) | async-done | bytes 4194320 | tf_op jit(solution)/shard_map/all_gather | solution.py:29
  341.5 15.2 %fusion.68 = (bf16[2048]{0:T(1024)(128)(2,1)}, bf16[1024,2048]{1,0:T(8,128)(2,1)S(1)}) fusion(f32[1024,2048]{1,0:T(8,128)} %fusion.79, f32[2048]{0:T(1024)S(1)} %copy-done.32, bf16[1024,1024]{1,0:T(8,128)(2,1)} %all-gather.21.cloned.1.call-done, bf16[2048,1024]{0,1:T(8,128)(2,1)} %all-gather.19.cloned.1.call-done), kind=kOutput, calls=%fused_computation.135 | convolution fusion | flops 4349491200 | bytes 18886656 | tf_op jit(solution)/shard_map/dot_general | solution.py:201
  364.6 11.3 convolution_convert_fusion.5
  376.4 18.6 %reduce-scatter.22.cloned.1.call-done = bf16[512,1024]{1,0:T(8,128)(2,1)} async-done(((bf16[1024,1024]{1,0:T(8,128)(2,1)}), bf16[512,1024]{1,0:T(8,128)(2,1)}) %reduce-scatter.22.cloned.1.call-update) | async-done | bytes 1048592 | tf_op jit(solution)/shard_map/reduce_scatter | solution.py:63
  397.4 31.6 %reduce-scatter.20.cloned.1.call-done = bf16[512,1024]{1,0:T(8,128)(2,1)} async-done(((bf16[1024,1024]{1,0:T(8,128)(2,1)}), bf16[512,1024]{1,0:T(8,128)(2,1)}) %reduce-scatter.20.cloned.1.call-update) | async-done | bytes 1048592 | tf_op jit(solution)/shard_map/reduce_scatter | solution.py:44
  436.4 32.6 %all-gather.23.cloned.1.call-done = bf16[1024,1024]{1,0:T(8,128)(2,1)} async-done(((bf16[512,1024]{1,0:T(8,128)(2,1)}), bf16[1024,1024]{1,0:T(8,128)(2,1)}) %all-gather.23.cloned.1.call-update) | async-done | bytes 2097168 | tf_op jit(solution)/shard_map/all_gather | solution.py:34
  496.7 10.0 multiply_reduce_fusion
  534.3 10.8 convolution_convert_fusion
  585.7 33.6 %all-reduce.2 = bf16[2048]{0:T(1024)(128)(2,1)S(1)} all-reduce(bf16[2048]{0:T(1024)(128)(2,1)S(1)} %copy-done.29), channel_id=12, replica_groups=mesh['dp'=16,'tensor'=2] {'dp'}, use_global_device_ids=true, to_apply=%region_33.34.clone | all-reduce | flops 2048 | bytes 8192
  619.8 22.7 %reduce-scatter.32.cloned.1.call-done = bf16[2048,64]{0,1:T(8,128)(2,1)} async-done(((bf16[2048,1024]{0,1:T(8,128)(2,1)}), bf16[2048,64]{0,1:T(8,128)(2,1)}) %reduce-scatter.32.cloned.1.call-update) | async-done | bytes 262160 | tf_op jit(solution)/shard_map/reduce_scatter | solution.py:214
  644.4 74.3 %reduce-scatter.30.cloned.1.call-done = bf16[64,2048]{1,0:T(8,128)(2,1)} async-done(((bf16[1024,2048]{1,0:T(8,128)(2,1)}), bf16[64,2048]{1,0:T(8,128)(2,1)}) %reduce-scatter.30.cloned.1.call-update) | async-done | bytes 262160 | tf_op jit(solution)/shard_map/reduce_scatter | solution.py:211
  720.4 56.2 %reduce-scatter.38.cloned.1.call-done = bf16[32,2]{1,0:T(8,128)(2,1)} async-done(((bf16[512,2]{1,0:T(8,128)(2,1)}), bf16[32,2]{1,0:T(8,128)(2,1)}) %reduce-scatter.38.cloned.1.call-update) | async-done | bytes 144
  778.0 58.6 %reduce-scatter.28.cloned.1.call-done = bf16[512,64]{0,1:T(8,128)(2,1)} async-done(((bf16[512,1024]{0,1:T(8,128)(2,1)}), bf16[512,64]{0,1:T(8,128)(2,1)}) %reduce-scatter.28.cloned.1.call-update) | async-done | bytes 65552 | tf_op jit(solution)/shard_map/reduce_scatter | solution.py:254
  838.1 133.7 %reduce-scatter.34.cloned.1.call-done = f32[32,2]{1,0:T(8,128)} async-done(((f32[1024,2]{1,0:T(8,128)}), f32[32,2]{1,0:T(8,128)}) %reduce-scatter.34.cloned.1.call-update) | async-done | bytes 272
  973.1 130.6 %reduce-scatter.36.cloned.1.call-done = f32[32,4]{1,0:T(8,128)} async-done(((f32[1024,4]{1,0:T(8,128)}), f32[32,4]{1,0:T(8,128)}) %reduce-scatter.36.cloned.1.call-update) | async-done | bytes 528
  1105.1 65.0 %reduce-scatter.26.cloned.1.call-done = bf16[64,3,512]{2,0,1:T(8,128)(2,1)} async-done(((bf16[1024,3,512]{2,0,1:T(8,128)(2,1)}), bf16[64,3,512]{2,0,1:T(8,128)(2,1)}) %reduce-scatter.26.cloned.1.call-update) | async-done | bytes 196624 | tf_op jit(solution)/shard_map/reduce_scatter | solution.py:251
  (203 shorter events, 176.1 us)
Async XLA Ops:
  7.2 51.0 %all-gather.11.cloned.1.call-start = ((), (), s32[]{:S(2)}) async-start(), calls=%async_computation.12 | async-start | bytes 3342336 | tf_op jit(solution)/shard_map/all_gather | solution.py:28
  7.9 84.3 %all-gather.9.cloned.1.call-start = ((), (), s32[]{:S(2)}) async-start(), calls=%async_computation.11 | async-start | bytes 3145728 | tf_op jit(solution)/shard_map/all_gather | solution.py:34
  11.6 51.2 %copy-start.21 = (f32[512]{0:T(512)}, f32[512]{0:T(512)S(1)}, u32[]{:S(2)}) copy-start(f32[512]{0:T(512)S(1)} %fusion.66) | copy-start | bytes 6148
  16.0 116.3 %all-gather.13.cloned.1.call-start = ((), (), s32[]{:S(2)}) async-start(), calls=%async_computation.13 | async-start | bytes 1114112 | tf_op jit(solution)/shard_map/all_gather | solution.py:29
  16.7 150.5 %reduce-scatter.18.cloned.1.call-start = ((), (), s32[]{:S(2)}) async-start(), calls=%async_computation.14 | async-start | bytes 3145728 | tf_op jit(solution)/shard_map/reduce_scatter | solution.py:44
  132.3 34.9 %copy-start.2 = (bf16[512,1024]{1,0:T(8,128)(2,1)S(1)}, bf16[512,1024]{1,0:T(8,128)(2,1)}, u32[]{:S(2)}) copy-start(bf16[512,1024]{1,0:T(8,128)(2,1)} %param.23) | copy-start | bytes 3145732
  136.3 83.8 %all-gather.17.cloned.1.call-start = ((), (), s32[]{:S(2)}) async-start(), calls=%async_computation.16 | async-start | bytes 4456448 | tf_op jit(solution)/shard_map/all_gather | solution.py:28
  136.9 116.9 %all-gather.15.cloned.1.call-start = ((), (), s32[]{:S(2)}) async-start(), calls=%async_computation.15 | async-start | bytes 3145728 | tf_op jit(solution)/shard_map/all_gather | solution.py:34
  172.4 116.2 %all-gather.21.cloned.1.call-start = ((), (), s32[]{:S(2)}) async-start(), calls=%async_computation.19 | async-start | bytes 3145728 | tf_op jit(solution)/shard_map/all_gather | solution.py:34
  173.1 168.4 %all-gather.19.cloned.1.call-start = ((), (), s32[]{:S(2)}) async-start(), calls=%async_computation.17 | async-start | bytes 4456448 | tf_op jit(solution)/shard_map/all_gather | solution.py:29
  173.9 167.6 %copy-start.32 = (f32[2048]{0:T(1024)S(1)}, f32[2048]{0:T(1024)}, u32[]{:S(2)}) copy-start(f32[2048]{0:T(1024)} %param.30) | copy-start | bytes 24580
  173.9 221.2 %reduce-scatter.22.cloned.1.call-start = ((), (), s32[]{:S(2)}) async-start(), calls=%async_computation.20 | async-start | bytes 3145728 | tf_op jit(solution)/shard_map/reduce_scatter | solution.py:63
  364.6 64.4 %reduce-scatter.20.cloned.1.call-start = ((), (), s32[]{:S(2)}) async-start(), calls=%async_computation.18 | async-start | bytes 3145728 | tf_op jit(solution)/shard_map/reduce_scatter | solution.py:44
  375.9 93.1 %all-gather.23.cloned.1.call-start = ((), (), s32[]{:S(2)}) async-start(), calls=%async_computation.21 | async-start | bytes 3145728 | tf_op jit(solution)/shard_map/all_gather | solution.py:34
  395.0 33.9 %copy-start.8 = (bf16[512,1024]{1,0:T(8,128)(2,1)S(1)}, bf16[512,1024]{1,0:T(8,128)(2,1)}, u32[]{:S(2)}) copy-start(bf16[512,1024]{1,0:T(8,128)(2,1)} %reduce-scatter.22.cloned.1.call-done) | copy-start | bytes 3145732
  432.4 36.6 %copy-start.31 = (bf16[512,1024]{0,1:T(8,128)(2,1)S(1)}, bf16[512,1024]{0,1:T(8,128)(2,1)}, u32[]{:S(2)}) copy-start(bf16[512,1024]{0,1:T(8,128)(2,1)} %all-gather.13.cloned.1.call-done) | copy-start | bytes 3145732
  435.8 130.2 %reduce-scatter.24.cloned.1.call-start = ((), (), s32[]{:S(2)}) async-start(), calls=%async_computation.22 | async-start | bytes 3145728 | tf_op jit(solution)/shard_map/reduce_scatter | solution.py:63
  534.0 108.6 %reduce-scatter.32.cloned.1.call-start = ((), (), s32[]{:S(2)}) async-start(), calls=%async_computation.26 | async-start | bytes 4456448 | tf_op jit(solution)/shard_map/reduce_scatter | solution.py:214
  545.1 173.6 %reduce-scatter.30.cloned.1.call-start = ((), (), s32[]{:S(2)}) async-start(), calls=%async_computation.25 | async-start | bytes 4456448 | tf_op jit(solution)/shard_map/reduce_scatter | solution.py:211
  554.5 222.1 %reduce-scatter.38.cloned.1.call-start = ((), (), s32[]{:S(2)}) async-start(), calls=%async_computation.29 | async-start | bytes 139264
  556.2 280.4 %reduce-scatter.28.cloned.1.call-start = ((), (), s32[]{:S(2)}) async-start(), calls=%async_computation.24 | async-start | bytes 1114112 | tf_op jit(solution)/shard_map/reduce_scatter | solution.py:254
  560.2 411.6 %reduce-scatter.34.cloned.1.call-start = ((), (), s32[]{:S(2)}) async-start(), calls=%async_computation.27 | async-start | bytes 540672
  571.5 532.2 %reduce-scatter.36.cloned.1.call-start = ((), (), s32[]{:S(2)}) async-start(), calls=%async_computation.28 | async-start | bytes 540672
  575.8 594.3 %reduce-scatter.26.cloned.1.call-start = ((), (), s32[]{:S(2)}) async-start(), calls=%async_computation.23 | async-start | bytes 3342336 | tf_op jit(solution)/shard_map/reduce_scatter | solution.py:251
  (37 other events, 240.6 us)
Sparse Core Ops, SparseCore 0:
  10.2 47.8 all-gather.10
  60.3 31.9 all-gather.8
  94.4 37.8 all-gather.12
  136.4 30.7 reduce-scatter.17
  169.5 50.5 all-gather.16
  222.1 31.6 all-gather.14
  255.4 33.1 all-gather.20
  290.9 50.5 all-gather.18
  364.7 30.3 reduce-scatter.21
  397.1 31.8 reduce-scatter.19
  435.9 33.1 all-gather.22
  534.1 31.8 reduce-scatter.23
  569.8 72.6 reduce-scatter.31
  646.8 71.8 reduce-scatter.29
  722.5 54.0 reduce-scatter.37
  780.1 56.4 reduce-scatter.27
  838.8 132.9 reduce-scatter.33
  973.9 129.7 reduce-scatter.35
  1108.0 62.0 reduce-scatter.25
where the time goes:
time: 1190 us; the launch traced here: 1180 us
  waiting for transfers between devices  904 us (76%)
  matrix products  143 us (12%)
  other arithmetic  53.5 us (4%)
  blocking collectives  33.6 us (3%)
  local copies, waits for them, and re-layouts  26.7 us (2%)
  between operations  15.6 us (1%)
    unnamed x22, waiting for transfers between devices  324 us
    all_gather x4, waiting for transfers between devices, spread_rows(): return lax.all_gather(rows, 'tensor', axis=0, tiled=True)  120 us
    all_gather x2, waiting for transfers between devices, collect(): lax.all_gather(first, 'dp', axis=0, tiled=True)  86.5 us
    reduce_scatter x1, waiting for transfers between devices, per_device(): lax.psum_scatter(in_grad.astype(jnp.bfloat16), 'dp', scatter_dimension=0,...  74.3 us
    all_gather x2, waiting for transfers between devices, collect(): lax.all_gather(second, 'dp', axis=1, tiled=True)  67.7 us
    reduce_scatter x1, waiting for transfers between devices, per_device(): lax.psum_scatter(qkv_grad.astype(jnp.bfloat16), 'dp', scatter_dimension=0...  65 us
    reduce_scatter x2, waiting for transfers between devices, project_sum(): lax.psum_scatter(jnp.dot(part, weight, preferred_element_type=jnp.float32...  61.9 us
    reduce_scatter x1, waiting for transfers between devices, per_device(): lax.psum_scatter(out_grad.astype(jnp.bfloat16), 'dp', scatter_dimension=1...  58.6 us
  transfers between devices with their start and end apart: 19, of which 19 were waited for; matrix products, arithmetic and copies ran while one was open for 10% of the time, Pallas kernels for 0%

commit v1 on v0

v1 whole, which is shorter than its diff:
```python
import math

import jax
import jax.numpy as jnp
from jax import lax
from jax.sharding import PartitionSpec as P

HEAD_DIM = 64


EPS = 1e-05
MASKED = -1000000000.0
GELU_C = 0.7978845608028654


def layer_norm(value, gain, shift):
    centre = value - jnp.mean(value, axis=-1, keepdims=True)
    spread = jnp.mean(centre * centre, axis=-1, keepdims=True)
    return centre * lax.rsqrt(spread + EPS) * gain + shift


def gelu_tanh(value):
    return 0.5 * value * (1.0 + jnp.tanh(GELU_C * (value + 0.044715 * value * value * value)))


def xor_send(value, axis, distance):
    size = lax.axis_size(axis)
    return lax.ppermute(value, axis, [(i, i ^ distance) for i in range(size)])


def join_shards(*shards):
    widths = [shard.shape[1] for shard in shards]
    full = lax.all_gather(jnp.concatenate(shards, axis=1), "dp", axis=0, tiled=True)
    parts = []
    start = 0
    for width in widths:
        parts.append(full[:, start : start + width])
        start += width
    return parts


def spread_rows(rows):
    blocks = [rows] + [xor_send(rows, "tensor", d) for d in range(1, lax.axis_size("tensor"))]
    return jnp.concatenate(blocks, axis=0)


def to_natural(values):
    ranks = lax.axis_size("tensor")
    me = lax.axis_index("tensor")
    rows = values.shape[0] // ranks
    if ranks == 2:
        own, other = values[:rows], values[rows:]
        return jnp.concatenate(
            [jnp.where(me == 0, own, other), jnp.where(me == 0, other, own)], axis=0
        )
    blocks = values.reshape(ranks, rows, *values.shape[1:])
    picked = [
        lax.dynamic_index_in_dim(blocks, jnp.bitwise_xor(me, j), 0, keepdims=False)
        for j in range(ranks)
    ]
    return jnp.concatenate(picked, axis=0)


def sum_to_owner(product, values):
    ranks = lax.axis_size("tensor")
    rows = values.shape[0] // ranks
    arrived = []
    for distance in range(1, ranks):
        part = product(values[distance * rows : (distance + 1) * rows]).astype(jnp.bfloat16)
        arrived.append(xor_send(part, "tensor", distance))
    total = product(values[:rows])
    for part in arrived:
        total = total + part.astype(jnp.float32)
    return total


def times(weight):
    return lambda rows: jnp.dot(rows, weight, preferred_element_type=jnp.float32)


def times_transposed(weight):
    return lambda rows: lax.dot_general(
        rows, weight, (((1,), (1,)), ((), ())), preferred_element_type=jnp.float32
    )


def halving_sum(value, axis, order, keep_dtype):
    size = lax.axis_size(axis)
    me = lax.axis_index(axis)
    left = [bit for bit in reversed(range(len(order)))]
    tail = (value.shape[0] // size,) + value.shape[1:]
    value = value.reshape((2,) * len(order) + tail)
    for step, bit in enumerate(order):
        place = left.index(bit)
        left.remove(bit)
        mine = lax.rem(me // (1 << bit), 2)
        send = lax.dynamic_index_in_dim(value, 1 - mine, place, keepdims=False)
        keep = lax.dynamic_index_in_dim(value, mine, place, keepdims=False)
        got = xor_send(send, axis, 1 << bit)
        value = keep.astype(jnp.float32) + got.astype(jnp.float32)
        if step < len(order) - 1:
            value = value.astype(keep_dtype)
    return value


def dp_orders():
    bits = lax.axis_size("dp").bit_length() - 1
    ahead = list(range(bits))
    return ahead, [0] + ahead[2:] + ahead[1:2]


def dp_sum(value, order):
    return halving_sum(value.astype(jnp.bfloat16), "dp", order, jnp.bfloat16)


def masks_for(seg, start, end):
    positions = jnp.arange(end, dtype=jnp.int32)
    same = seg[start:end, None] == seg[None, :end]
    causal = positions[start:end, None] >= positions[None, :end]
    return same & causal


def attention_forward(query, key, value, segments, scale):
    length = query.shape[1]
    block = min(512, length)
    blocks = length // block

    def one_seq(items):
        q_seq, k_seq, v_seq, seg = items
        outs = []
        sums = []
        for index in range(blocks):
            start = index * block
            end = start + block
            allowed = masks_for(seg, start, end)
            scores = (
                jnp.einsum(
                    "qhd,khd->hqk",
                    q_seq[start:end],
                    k_seq[:end],
                    preferred_element_type=jnp.float32,
                )
                * scale
            )
            scores = jnp.where(allowed[None], scores, MASKED)
            top = jnp.max(scores, axis=-1, keepdims=True)
            expo = jnp.exp(scores - top)
            total = jnp.sum(expo, axis=-1, keepdims=True)
            probs = (expo / total).astype(jnp.bfloat16)
            outs.append(
                jnp.einsum("hqk,khd->qhd", probs, v_seq[:end], preferred_element_type=jnp.float32)
            )
            sums.append((top + jnp.log(total))[..., 0])
        return (jnp.concatenate(outs, 0), jnp.concatenate(sums, 1))

    return lax.map(one_seq, (query, key, value, segments))


def attention_backward(query, key, value, segments, logsum, grad_att, scale):
    length = query.shape[1]
    block = min(512, length)
    blocks = length // block

    def one_seq(items):
        q_seq, k_seq, v_seq, seg, lse, do_seq = items
        dq_parts = []
        key_grad = jnp.zeros(k_seq.shape, jnp.float32)
        value_grad = jnp.zeros(v_seq.shape, jnp.float32)
        for index in range(blocks):
            start = index * block
            end = start + block
            allowed = masks_for(seg, start, end)
            q_rows = q_seq[start:end]
            do_rows = do_seq[start:end]
            scores = (
                jnp.einsum("qhd,khd->hqk", q_rows, k_seq[:end], preferred_element_type=jnp.float32)
                * scale
            )
            scores = jnp.where(allowed[None], scores, MASKED)
            probs = jnp.exp(scores - lse[:, start:end, None])
            probs_low = probs.astype(jnp.bfloat16)
            dprobs = jnp.einsum(
                "qhd,khd->hqk", do_rows, v_seq[:end], preferred_element_type=jnp.float32
            )
            inner = jnp.sum(dprobs * probs, axis=-1, keepdims=True)
            dscores = (probs * (dprobs - inner)).astype(jnp.bfloat16)
            dq_parts.append(
                jnp.einsum("hqk,khd->qhd", dscores, k_seq[:end], preferred_element_type=jnp.float32)
                * scale
            )
            key_grad = key_grad.at[:end].add(
                jnp.einsum("hqk,qhd->khd", dscores, q_rows, preferred_element_type=jnp.float32)
                * scale
            )
            value_grad = value_grad.at[:end].add(
                jnp.einsum("hqk,qhd->khd", probs_low, do_rows, preferred_element_type=jnp.float32)
            )
        return (jnp.concatenate(dq_parts, 0), key_grad, value_grad)

    return lax.map(one_seq, (query, key, value, segments, logsum, grad_att))


def per_device(
    tokens, gains, shifts, w_qkv, bias_qv, w_out, w_in, bias_in, w_down, segments, grad_output
):
    seqs, length = segments.shape
    scale = 1.0 / math.sqrt(HEAD_DIM)
    order_a, order_b = dp_orders()
    shard = w_qkv.shape[0]
    local_width = w_qkv.shape[2]
    ranks = lax.axis_size("tensor")
    my_rank = lax.axis_index("tensor")
    rows_local = tokens.shape[0]
    qkv_flat, out_turned = join_shards(w_qkv.reshape(shard, 3 * local_width), w_out.T)
    in_full, down_turned = join_shards(w_in, w_down.T)
    heads = local_width // HEAD_DIM
    rows_in = tokens.astype(jnp.float32)
    normed_one = layer_norm(rows_in, gains[0], shifts[0])
    full_a = spread_rows(normed_one.astype(jnp.bfloat16))
    full_dy = spread_rows(grad_output)
    total = full_a.shape[0]
    bias_all = jnp.concatenate([bias_qv[0], jnp.zeros_like(bias_qv[0]), bias_qv[1]])
    mixed = jnp.dot(full_a, qkv_flat, preferred_element_type=jnp.float32) + bias_all
    shaped = to_natural(mixed.astype(jnp.bfloat16)).reshape(seqs, length, 3, heads, HEAD_DIM)
    query = shaped[:, :, 0]
    key = shaped[:, :, 1]
    value = shaped[:, :, 2]
    attended, logsum = attention_forward(query, key, value, segments, scale)
    attended_low = to_natural(attended.reshape(total, local_width).astype(jnp.bfloat16))
    middle = rows_in + sum_to_owner(times_transposed(out_turned), attended_low) + shifts[1]
    normed_two = layer_norm(middle, gains[1], shifts[2])
    full_m = spread_rows(normed_two.astype(jnp.bfloat16))
    hidden_grad = jnp.dot(full_dy, down_turned, preferred_element_type=jnp.float32)
    hidden_pre = jnp.dot(full_m, in_full, preferred_element_type=jnp.float32) + bias_in
    hidden_low = gelu_tanh(hidden_pre).astype(jnp.bfloat16)
    gelu_out, gelu_back = jax.vjp(gelu_tanh, hidden_pre)
    pre_grad = gelu_back(hidden_grad)[0].astype(jnp.bfloat16)
    normed_two_grad = sum_to_owner(times_transposed(in_full), pre_grad)
    result = middle + sum_to_owner(times_transposed(down_turned), hidden_low) + shifts[3]
    output = result.astype(jnp.bfloat16)
    grad_rows = grad_output.astype(jnp.float32)
    bias_in_part = jnp.sum(pre_grad, axis=0, dtype=jnp.float32)
    down_grad = lax.dot_general(
        full_dy, hidden_low, (((0,), (0,)), ((), ())), preferred_element_type=jnp.float32
    )
    in_grad = lax.dot_general(
        full_m, pre_grad, (((0,), (0,)), ((), ())), preferred_element_type=jnp.float32
    )
    ff_in = dp_sum(in_grad, order_a)
    ff_down = dp_sum(down_grad, order_b).T
    norm_two_out, norm_two_back = jax.vjp(layer_norm, middle, gains[1], shifts[2])
    middle_part, gain_two_grad, shift_two_grad = norm_two_back(normed_two_grad)
    middle_grad = grad_rows + middle_part
    branch_low = middle_grad.astype(jnp.bfloat16)
    full_branch = spread_rows(branch_low)
    attended_grad = jnp.dot(full_branch, out_turned, preferred_element_type=jnp.float32)
    attended_grad_low = to_natural(attended_grad.astype(jnp.bfloat16))
    out_grad = lax.dot_general(
        full_branch, attended_low, (((0,), (0,)), ((), ())), preferred_element_type=jnp.float32
    )
    att_out = dp_sum(out_grad, order_b).T
    query_grad, key_grad, value_grad = attention_backward(
        query,
        key,
        value,
        segments,
        logsum,
        attended_grad_low.reshape(seqs, length, heads, HEAD_DIM),
        scale,
    )
    mixed_grad = jnp.concatenate(
        [
            part.astype(jnp.bfloat16).reshape(total, local_width)
            for part in (query_grad, key_grad, value_grad)
        ],
        axis=1,
    )
    mixed_flat = to_natural(mixed_grad)
    normed_one_grad = sum_to_owner(times_transposed(qkv_flat), mixed_flat)
    qkv_grad = lax.dot_general(
        full_a, mixed_flat, (((0,), (0,)), ((), ())), preferred_element_type=jnp.float32
    )
    half = 3 * local_width // 2
    att_qkv = jnp.concatenate(
        [dp_sum(qkv_grad[:, :half], order_a), dp_sum(qkv_grad[:, half:], order_b)], axis=1
    ).reshape(shard, 3, local_width)
    mixed_bias = jnp.sum(mixed_flat, axis=0, dtype=jnp.float32)
    bias_qv_part = jnp.stack([mixed_bias[:local_width], mixed_bias[2 * local_width :]])
    norm_one_out, norm_one_back = jax.vjp(layer_norm, rows_in, gains[0], shifts[0])
    input_part, gain_one_grad, shift_one_grad = norm_one_back(normed_one_grad)
    input_grad = (middle_grad + input_part).astype(jnp.bfloat16)
    norm_parts = jnp.stack(
        [
            gain_one_grad,
            gain_two_grad,
            shift_one_grad,
            jnp.sum(branch_low, axis=0, dtype=jnp.float32),
            shift_two_grad,
            jnp.sum(grad_rows, axis=0),
        ]
    )
    groups = lax.axis_size("dp")
    width = norm_parts.shape[1] // (groups * ranks)
    norm_packed = norm_parts.reshape(6, groups, ranks, width).transpose(1, 2, 0, 3)
    norm_packed = norm_packed.reshape(groups, ranks, 6 * width)
    bias_packed = jnp.concatenate(
        [
            bias_qv_part.reshape(2, groups, -1).transpose(1, 0, 2).reshape(groups, -1),
            bias_in_part.reshape(groups, -1),
        ],
        axis=1,
    )
    mine = jnp.arange(ranks, dtype=jnp.int32)[None, :, None] == my_rank
    bias_spread = jnp.where(mine, bias_packed[:, None, :], 0.0)
    packed = jnp.concatenate([norm_packed, bias_spread], axis=2)
    packed = packed.transpose(1, 0, 2)
    rank_bits = list(range(ranks.bit_length() - 1))
    summed = halving_sum(packed, "tensor", rank_bits, jnp.float32)[0]
    summed = halving_sum(summed, "dp", order_a, jnp.float32)[0]
    norm_sums = summed[: 6 * width].reshape(6, width)
    gains_grad, shifts_grad = norm_sums[:2], norm_sums[2:]
    qv_width = bias_qv_part.shape[1] // groups
    att_bias = summed[6 * width : 6 * width + 2 * qv_width].reshape(2, qv_width)
    ff_bias = summed[6 * width + 2 * qv_width :]
    return (
        output,
        input_grad,
        gains_grad,
        shifts_grad,
        att_qkv,
        att_bias,
        att_out,
        ff_in,
        ff_bias,
        ff_down,
    )


def solution(mesh):
    placed = (
        P(("dp", "tensor"), None),
        P(),
        P(),
        P("dp", None, "tensor"),
        P(None, "tensor"),
        P("tensor", "dp"),
        P("dp", "tensor"),
        P("tensor"),
        P("tensor", "dp"),
        P("dp", None),
        P(("dp", "tensor"), None),
    )
    return jax.shard_map(
        per_device,
        mesh=mesh,
        in_specs=placed,
        out_specs=(
            P(("dp", "tensor"), None),
            P(("dp", "tensor"), None),
            P(None, ("dp", "tensor")),
            P(None, ("dp", "tensor")),
            P("dp", None, "tensor"),
            P(None, ("tensor", "dp")),
            P("tensor", "dp"),
            P("dp", "tensor"),
            P(("tensor", "dp")),
            P("tensor", "dp"),
        ),
        check_vma=False,
    )
```

time: 1190 us -> 494 us (0.42)
  waiting for transfers between devices: 904 us -> 210 us
  blocking collectives: 33.6 us -> 0 us
  starting transfers between devices: 1.64 us -> 31.6 us
  local copies, waits for them, and re-layouts: 26.7 us -> 49.5 us
  matrix products: 143 us -> 125 us
    unnamed x22 -> x2, waiting for transfers between devices: 324 us -> 0.03 us
    reduce_scatter x8 -> x0, waiting for transfers between devices: 307 us -> none  [the longest x1 74.3 us: per_device(): lax.psum_scatter(in_grad.astype(jnp.bfloat16), 'dp', scatter_dimension=0,...]
    all_gather x8 -> x2, waiting for transfers between devices: 274 us -> 24.3 us  [join_shards(): lax.all_gather(jnp.concatenate(shards, axis=1), 'dp', axis=0, tiled=True)]
    ppermute x0 -> x33, waiting for transfers between devices: none -> 185 us  [xor_send(): return lax.ppermute(value, axis, [(i, i ^ distance) for i in range(size)])]
    unnamed x1 -> x0, blocking collectives: 33.6 us -> none
    ppermute x0 -> x33, starting transfers between devices: none -> 31.5 us  [xor_send(): return lax.ppermute(value, axis, [(i, i ^ distance) for i in range(size)])]
    dot_general x9 -> x13, matrix products: 64.6 us -> 57.5 us  [the longest x8 29 us: times_transposed(): lax.dot_general(rows, weight, (((1,), (1,)), ((), ())), preferred_element...]
  transfers between devices with their start and end apart: 19 -> 35, of which waited for: 19 -> 18; matrix products, arithmetic and copies ran while one was open for 10% -> 41% of each run, Pallas kernels for 0% -> 0%
where the time goes in v1:
time: 494 us; the launch traced here: 491 us
  waiting for transfers between devices  210 us (43%)
  matrix products  125 us (25%)
  other arithmetic  59.5 us (12%)
  local copies, waits for them, and re-layouts  49.5 us (10%)
  starting transfers between devices  31.6 us (6%)
  between operations  15.5 us (3%)
    ppermute x33, waiting for transfers between devices, xor_send(): return lax.ppermute(value, axis, [(i, i ^ distance) for i in range(size)])  185 us
    ppermute x33, starting transfers between devices, xor_send(): return lax.ppermute(value, axis, [(i, i ^ distance) for i in range(size)])  31.5 us
    dot_general x8, matrix products, times_transposed(): lax.dot_general(rows, weight, (((1,), (1,)), ((), ())), preferred_element...  29 us
    all_gather x2, waiting for transfers between devices, join_shards(): lax.all_gather(jnp.concatenate(shards, axis=1), 'dp', axis=0, tiled=True)  24.3 us
    unnamed x172, local copies, waits for them, and re-layouts  14.9 us
    convert_element_type x15, other arithmetic, halving_sum(): value = value.astype(keep_dtype)  14.7 us
    convert_element_type x2, other arithmetic, one_seq(): dscores = (probs * (dprobs - inner)).astype(jnp.bfloat16)  14.5 us
    dot_general x1, matrix products, per_device(): jnp.dot(full_dy, down_turned, preferred_element_type=jnp.float32)  13.4 us
  transfers between devices with their start and end apart: 35, of which 18 were waited for; matrix products, arithmetic and copies ran while one was open for 41% of the time, Pallas kernels for 0%

profile of v1, /device:TPU:0, one launch (start us, length us, event | category | flops | bytes accessed | tf_op | source)
XLA Modules:
  0.0 490.7 jit_solution(2536031003911943238)
XLA Ops:
  18.3 21.5 %collective-permute-done = bf16[512,1024]{1,0:T(8,128)(2,1)S(1)} collective-permute-done((bf16[512,1024]{1,0:T(8,128)(2,1)S(1)}, bf16[512,1024]{1,0:T(8,128)(2,1)S(1)}, u32[]{:S(2)}, u32[]{:S(2)}) %collective-permute-start) | collective-permute-done | bytes 1048608 | tf_op jit(solution)/shard_map/ppermute | solution.py:28
  39.8 24.3 %all-gather.3.cloned.1.call-done = bf16[1024,2048]{1,0:T(8,128)(2,1)} async-done(((bf16[64,2048]{1,0:T(8,128)(2,1)}), bf16[1024,2048]{1,0:T(8,128)(2,1)}) %all-gather.3.cloned.1.call-update) | async-done | bytes 4194320 | tf_op jit(solution)/shard_map/all_gather | solution.py:33
  64.1 6.5 %add_convert_fusion = bf16[1024,1536]{1,0:T(8,128)(2,1)S(1)} fusion(f32[1536]{0:T(1024)S(1)} %pad_maximum_fusion.17, bf16[1024,2048]{1,0:T(8,128)(2,1)} %all-gather.3.cloned.1.call-done, bf16[512,1024]{1,0:T(8,128)(2,1)S(1)} %collective-permute-done, bf16[512,1024]{1,0:T(8,128)(2,1)S(1)} %fusion.46), kind=kOutput, calls=%fused_computation.32 | convolution fusion | flops 3228565504 | bytes 8394752 | tf_op jit(solution)/shard_map/dot_general | solution.py:223
  92.5 5.3 %fusion.85 = bf16[8,64,512]{2,1,0:T(8,128)(2,1)} fusion(f32[8,512,1024]{2,1,0:T(8,128)S(1)} %get-tuple-element.219, f32[8,512]{1,0:T(8,128)S(1)} %fusion, f32[8,512]{1,0:T(8,128)S(1)} %get-tuple-element.218, bf16[1,1024,3,8,64]{1,4,3,2,0:T(8,128)(2,1)} %bitcast.269), kind=kOutput, calls=%fused_computation.135 | convolution fusion | flops 549715968 | bytes 18382848 | tf_op jit(solution)/shard_map/while/body/eval_jaxpr/hqk,khd->qhd/dot_general | solution.py:151
  104.3 24.0 %collective-permute-done.1 = bf16[512,1024]{1,0:T(8,128)(2,1)S(1)} collective-permute-done((bf16[512,1024]{1,0:T(8,128)(2,1)S(1)}, bf16[512,1024]{1,0:T(8,128)(2,1)S(1)}, u32[]{:S(2)}, u32[]{:S(2)}) %collective-permute-start.1) | collective-permute-done | bytes 1048608 | tf_op jit(solution)/shard_map/ppermute | solution.py:28
  133.1 17.6 %collective-permute-done.4 = bf16[512,1024]{1,0:T(8,128)(2,1)S(1)} collective-permute-done((bf16[512,1024]{1,0:T(8,128)(2,1)S(1)}, bf16[512,1024]{1,0:T(8,128)(2,1)S(1)}, u32[]{:S(2)}, u32[]{:S(2)}) %collective-permute-start.4) | collective-permute-done | bytes 1048608 | tf_op jit(solution)/shard_map/ppermute | solution.py:28
  152.8 19.8 %collective-permute-done.2 = bf16[512,1024]{1,0:T(8,128)(2,1)} collective-permute-done((bf16[512,1024]{1,0:T(8,128)(2,1)S(1)}, bf16[512,1024]{1,0:T(8,128)(2,1)}, u32[]{:S(2)}, u32[]{:S(2)}) %collective-permute-start.2) | collective-permute-done | bytes 1048608 | tf_op jit(solution)/shard_map/ppermute | solution.py:28
  172.7 10.2 %multiply_convert_fusion.2 = (bf16[1024,2048]{1,0:T(8,128)(2,1)S(1)}, f32[1024,2048]{1,0:T(8,128)}) fusion(f32[2048]{0:T(1024)S(1)} %copy-done.69, bf16[1024,4096]{1,0:T(8,128)(2,1)} %all-gather.5.cloned.1.call-done, bf16[512,1024]{1,0:T(8,128)(2,1)} %collective-permute-done.2, bf16[512,1024]{1,0:T(8,128)(2,1)S(1)} %add_convert_fusion.3), kind=kOutput, calls=%fused_computation.24 | convolution fusion | flops 4320133120 | bytes 18882560 | tf_op jit(solution)/shard_map/dot_general | solution.py:234
  192.6 13.4 %convert_reduce_fusion = (f32[2048]{0:T(1024)S(1)}, bf16[1024,2048]{1,0:T(8,128)(2,1)S(1)}) fusion(bf16[1024,1024]{1,0:T(8,128)(2,1)S(1)} %copy-done.31, bf16[1024,4096]{1,0:T(8,128)(2,1)S(1)} %copy-done.62, f32[1024,2048]{1,0:T(8,128)} %get-tuple-element.224, f32[2048]{0:T(1024)S(1)} %copy-done.69), kind=kOutput, calls=%fused_computation.19 | convolution fusion | flops 4351588352 | bytes 18890752 | tf_op jit(solution)/shard_map/dot_general | solution.py:233
  209.0 6.3 %convolution_convert_fusion.2 = bf16[1024,2048]{1,0:T(8,128)(2,1)S(1)} fusion(bf16[1024,2048]{1,0:T(8,128)(2,1)S(1)} %get-tuple-element.231, bf16[512,1024]{1,0:T(8,128)(2,1)} %collective-permute-done.2, bf16[512,1024]{1,0:T(8,128)(2,1)S(1)} %add_convert_fusion.3), kind=kOutput, calls=%fused_computation.42 | convolution fusion | flops 4301258752 | bytes 10485760 | tf_op jit(solution)/shard_map/dot_general | solution.py:246
  221.3 12.2 %collective-permute-done.5 = bf16[512,1024]{1,0:T(8,128)(2,1)S(1)} collective-permute-done((bf16[512,1024]{1,0:T(8,128)(2,1)S(1)}, bf16[512,1024]{1,0:T(8,128)(2,1)S(1)}, u32[]{:S(2)}, u32[]{:S(2)}) %collective-permute-start.5) | collective-permute-done | bytes 1048608 | tf_op jit(solution)/shard_map/ppermute | solution.py:28
  233.5 6.9 %multiply_reduce_fusion.2 = (f32[1024]{0:T(1024)S(1)}, f32[512]{0:T(512)S(1)}, f32[1024]{0:T(1024)S(1)}, f32[512,1024]{1,0:T(8,128)}) fusion(f32[512,1024]{1,0:T(8,128)S(1)} %copy-done.13, f32[512]{0:T(512)S(1)} %fusion.126, f32[512]{0:T(512)S(1)} %broadcast_multiply_fusion, bf16[512,1024]{1,0:T(8,128)(2,1)S(1)} %collective-permute-done.5, ...), kind=kOutput, calls=%fused_computation.102 | convolution fusion | flops 2152723968 | bytes 11552768 | tf_op jit(solution)/shard_map/dot_general | solution.py:82
  241.7 8.4 %fusion.138 = (f32[512]{0:T(512)S(1)}, f32[512,1024]{1,0:T(8,128)S(1)}, bf16[512,1024]{1,0:T(8,128)(2,1)}) fusion(f32[512]{0:T(512)S(1)} %multiply_multiply_fusion.3, f32[512,1024]{1,0:T(8,128)} %copy-done.12, f32[512]{0:T(512)S(1)} %broadcast_multiply_fusion, f32[512]{0:T(512)S(1)} %fusion.126, f32[1024]{0:T(1024)S(1)} %bitcast.307, ...), kind=kOutput, calls=%fused_computation.284 | convolution fusion | flops 2154823168 | bytes 15745024 | tf_op jit(solution)/shard_map/dot_general | solution.py:82
  264.7 13.0 %collective-permute-done.6 = bf16[512,1024]{1,0:T(8,128)(2,1)S(1)} collective-permute-done((bf16[512,1024]{1,0:T(8,128)(2,1)}, bf16[512,1024]{1,0:T(8,128)(2,1)S(1)}, u32[]{:S(2)}, u32[]{:S(2)}) %collective-permute-start.6) | collective-permute-done | bytes 1048608 | tf_op jit(solution)/shard_map/ppermute | solution.py:28
  300.1 10.1 %multiply_reduce_fusion = (f32[8,512]{1,0:T(8,128)}, f32[8,512,1024]{2,1,0:T(8,128)}) fusion(f32[8,512,1024]{2,1,0:T(8,128)S(1)} %bitcast.265, f32[8,512]{1,0:T(8,128)} %log_add_fusion, bf16[512,8,64]{0,2,1:T(8,128)(2,1)} %bitcast.281, bf16[1,1024,3,8,64]{1,4,3,2,0:T(8,128)(2,1)} %bitcast.274), kind=kOutput, calls=%fused_computation.1 | convolution fusion | flops 549449728 | bytes 35160064 | tf_op jit(solution)/shard_map/while/body/eval_jaxpr/qhd,khd->hqk/dot_general | solution.py:182
  310.1 5.0 %fusion.57 = bf16[1024,8,64]{0,2,1:T(8,128)(2,1)} fusion(f32[512,8,64]{0,2,1:T(8,128)} %fusion.77, bf16[512,8,64]{0,2,1:T(8,128)(2,1)} %bitcast.282, f32[8,512,1024]{2,1,0:T(8,128)S(1)} %bitcast.265, f32[8,512]{1,0:T(8,128)} %log_add_fusion), kind=kOutput, calls=%fused_computation.96 | convolution fusion | flops 546308096 | bytes 19415040 | tf_op jit(solution)/shard_map/while/body/eval_jaxpr/hqk,qhd->khd/dot_general | solution.py:196
  318.7 11.9 %multiply_convert_fusion = bf16[8,512,1024]{2,1,0:T(8,128)(2,1)S(1)} fusion(f32[8,512,1024]{2,1,0:T(8,128)} %get-tuple-element.228, f32[8,512,1024]{2,1,0:T(8,128)} %copy-done, f32[8,512]{1,0:T(8,128)S(1)} %copy-done.41, f32[8,512]{1,0:T(8,128)S(1)} %copy-done.33), kind=kLoop, calls=%fused_computation | loop fusion | flops 16777216 | bytes 41975808 | tf_op jit(solution)/shard_map/while/body/eval_jaxpr/convert_element_type | solution.py:186
  343.5 5.5 %convolution_convert_fusion = bf16[1024,1536]{1,0:T(8,128)(2,1)S(1)} fusion(bf16[512,1536]{1,0:T(8,128)(2,1)} %copy-done.16, bf16[512,1536]{1,0:T(8,128)(2,1)S(1)} %get-tuple-element.186, bf16[512,1024]{1,0:T(8,128)(2,1)} %copy-done.65, bf16[512,1024]{1,0:T(8,128)(2,1)} %copy-done.29), kind=kOutput, calls=%fused_computation.40 | convolution fusion | flops 3233284096 | bytes 8388608 | tf_op jit(solution)/shard_map/dot_general | solution.py:280
  360.3 6.3 %collective-permute-done.22 = bf16[2,2,64,512]{3,2,1,0:T(8,128)(2,1)S(1)} collective-permute-done((bf16[2,2,64,512]{3,2,1,0:T(8,128)(2,1)S(1)}, bf16[2,2,64,512]{3,2,1,0:T(8,128)(2,1)S(1)}, u32[]{:S(2)}, u32[]{:S(2)}) %collective-permute-start.22) | collective-permute-done | bytes 262176 | tf_op jit(solution)/shard_map/ppermute | solution.py:28
  377.0 14.2 %collective-permute-done.7 = bf16[512,1024]{1,0:T(8,128)(2,1)S(1)} collective-permute-done((bf16[512,1024]{1,0:T(8,128)(2,1)S(1)}, bf16[512,1024]{1,0:T(8,128)(2,1)S(1)}, u32[]{:S(2)}, u32[]{:S(2)}) %collective-permute-start.7) | collective-permute-done | bytes 1048608 | tf_op jit(solution)/shard_map/ppermute | solution.py:28
  414.1 10.4 %collective-permute-done.11 = f32[2,1,384]{2,1,0:T(1,128)S(1)} collective-permute-done((f32[2,1,384]{2,1,0:T(1,128)S(1)}, f32[2,1,384]{2,1,0:T(1,128)S(1)}, u32[]{:S(2)}, u32[]{:S(2)}) %collective-permute-start.11) | collective-permute-done | bytes 3104 | tf_op jit(solution)/shard_map/ppermute | solution.py:28
  436.0 8.2 %collective-permute-done.15 = bf16[2,64,768]{2,1,0:T(8,128)(2,1)S(1)} collective-permute-done((bf16[2,64,768]{2,1,0:T(8,128)(2,1)S(1)}, bf16[2,64,768]{2,1,0:T(8,128)(2,1)S(1)}, u32[]{:S(2)}, u32[]{:S(2)}) %collective-permute-start.15) | collective-permute-done | bytes 196640 | tf_op jit(solution)/shard_map/ppermute | solution.py:28
  446.6 15.1 %collective-permute-done.19 = bf16[2,64,768]{2,1,0:T(8,128)(2,1)S(1)} collective-permute-done((bf16[2,64,768]{2,1,0:T(8,128)(2,1)S(1)}, bf16[2,64,768]{2,1,0:T(8,128)(2,1)S(1)}, u32[]{:S(2)}, u32[]{:S(2)}) %collective-permute-start.19) | collective-permute-done | bytes 196640 | tf_op jit(solution)/shard_map/ppermute | solution.py:28
  469.5 12.5 %collective-permute-done.28 = bf16[64,2048]{1,0:T(8,128)(2,1)S(1)} collective-permute-done((bf16[64,2048]{1,0:T(8,128)(2,1)S(1)}, bf16[64,2048]{1,0:T(8,128)(2,1)S(1)}, u32[]{:S(2)}, u32[]{:S(2)}) %collective-permute-start.28) | collective-permute-done | bytes 262176 | tf_op jit(solution)/shard_map/ppermute | solution.py:28
  (376 shorter events, 186.9 us)
Async XLA Ops:
  7.2 56.9 %all-gather.3.cloned.1.call-start = ((), (), s32[]{:S(2)}) async-start(), calls=%async_computation | async-start | bytes 4456448 | tf_op jit(solution)/shard_map/all_gather | solution.py:33
  9.9 162.8 %all-gather.5.cloned.1.call-start = ((), (), s32[]{:S(2)}) async-start(), calls=%async_computation.1 | async-start | bytes 8912896 | tf_op jit(solution)/shard_map/all_gather | solution.py:33
  13.6 26.2 %collective-permute-start = (bf16[512,1024]{1,0:T(8,128)(2,1)S(1)}, bf16[512,1024]{1,0:T(8,128)(2,1)S(1)}, u32[]{:S(2)}, u32[]{:S(2)}) collective-permute-start(bf16[512,1024]{1,0:T(8,128)(2,1)S(1)} %fusion.46), channel_id=1, source_target_pairs={{0,1},{1,0},{2,3},{3,2},{4,5},{5,4},{6,7},{7,6},{8,9},{9,8},{10,11... | collective-permute-start | bytes 3145736 | tf_op jit(solution)/shard_map/ppermute | solution.py:28
  102.2 26.1 %collective-permute-start.1 = (bf16[512,1024]{1,0:T(8,128)(2,1)S(1)}, bf16[512,1024]{1,0:T(8,128)(2,1)S(1)}, u32[]{:S(2)}, u32[]{:S(2)}) collective-permute-start(bf16[512,1024]{1,0:T(8,128)(2,1)S(1)} %convolution_convert_fusion.5), channel_id=1, source_target_pairs={{0,1},{1,0},{2,3},{3,2},{4,5},{5,4},{6,7},{7,6},{8,9},{9,8},{10,11... | collective-permute-start | bytes 3145736 | tf_op jit(solution)/shard_map/ppermute | solution.py:28
  103.7 47.0 %collective-permute-start.4 = (bf16[512,1024]{1,0:T(8,128)(2,1)S(1)}, bf16[512,1024]{1,0:T(8,128)(2,1)S(1)}, u32[]{:S(2)}, u32[]{:S(2)}) collective-permute-start(bf16[512,1024]{1,0:T(8,128)(2,1)S(1)} %copy-done.8), channel_id=1, source_target_pairs={{0,1},{1,0},{2,3},{3,2},{4,5},{5,4},{6,7},{7,6},{8,9},{9,8},{10,11... | collective-permute-start | bytes 3145736 | tf_op jit(solution)/shard_map/ppermute | solution.py:28
  131.0 41.6 %collective-permute-start.2 = (bf16[512,1024]{1,0:T(8,128)(2,1)S(1)}, bf16[512,1024]{1,0:T(8,128)(2,1)}, u32[]{:S(2)}, u32[]{:S(2)}) collective-permute-start(bf16[512,1024]{1,0:T(8,128)(2,1)S(1)} %add_convert_fusion.3), channel_id=1, source_target_pairs={{0,1},{1,0},{2,3},{3,2},{4,5},{5,4},{6,7},{7,6},{8,9},{9,8},{10,11... | collective-permute-start | bytes 3145736 | tf_op jit(solution)/shard_map/ppermute | solution.py:28
  186.3 55.4 %collective-permute-start.3 = (bf16[512,1024]{1,0:T(8,128)(2,1)}, bf16[512,1024]{1,0:T(8,128)(2,1)}, u32[]{:S(2)}, u32[]{:S(2)}) collective-permute-start(bf16[512,1024]{1,0:T(8,128)(2,1)} %fusion.72), channel_id=1, source_target_pairs={{0,1},{1,0},{2,3},{3,2},{4,5},{5,4},{6,7},{7,6},{8,9},{9,8},{10,11... | collective-permute-start | bytes 3145736 | tf_op jit(solution)/shard_map/ppermute | solution.py:28
  208.4 25.1 %collective-permute-start.5 = (bf16[512,1024]{1,0:T(8,128)(2,1)S(1)}, bf16[512,1024]{1,0:T(8,128)(2,1)S(1)}, u32[]{:S(2)}, u32[]{:S(2)}) collective-permute-start(bf16[512,1024]{1,0:T(8,128)(2,1)S(1)} %fusion.67), channel_id=1, source_target_pairs={{0,1},{1,0},{2,3},{3,2},{4,5},{5,4},{6,7},{7,6},{8,9},{9,8},{10,11... | collective-permute-start | bytes 3145736 | tf_op jit(solution)/shard_map/ppermute | solution.py:28
  220.8 34.2 %collective-permute-start.25 = (bf16[2,2,2,64,2048]{4,3,0,1,2:T(8,128)(2,1)}, bf16[2,2,2,64,2048]{4,3,0,1,2:T(8,128)(2,1)}, u32[]{:S(2)}, u32[]{:S(2)}) collective-permute-start(bf16[2,2,2,64,2048]{4,3,0,1,2:T(8,128)(2,1)} %bitcast.259), channel_id=1, source_target_pairs={{0,2},{2,0},{4,6},{6,4},{8,10},{10,8},{12,14},{14,12},{16,18},{18,... | collective-permute-start | bytes 6291464 | tf_op jit(solution)/shard_map/ppermute | solution.py:28
  220.8 38.4 %collective-permute-start.29 = (bf16[2,2,2,64,2048]{4,3,2,0,1:T(8,128)(2,1)}, bf16[2,2,2,64,2048]{4,3,2,0,1:T(8,128)(2,1)}, u32[]{:S(2)}, u32[]{:S(2)}) collective-permute-start(bf16[2,2,2,64,2048]{4,3,2,0,1:T(8,128)(2,1)} %bitcast.258), channel_id=1, source_target_pairs={{0,2},{2,0},{4,6},{6,4},{8,10},{10,8},{12,14},{14,12},{16,18},{18,... | collective-permute-start | bytes 6291464 | tf_op jit(solution)/shard_map/ppermute | solution.py:28
  253.4 24.3 %collective-permute-start.6 = (bf16[512,1024]{1,0:T(8,128)(2,1)}, bf16[512,1024]{1,0:T(8,128)(2,1)S(1)}, u32[]{:S(2)}, u32[]{:S(2)}) collective-permute-start(bf16[512,1024]{1,0:T(8,128)(2,1)} %get-tuple-element.174), channel_id=1, source_target_pairs={{0,1},{1,0},{2,3},{3,2},{4,5},{5,4},{6,7},{7,6},{8,9},{9,8},{10,11... | collective-permute-start | bytes 3145736 | tf_op jit(solution)/shard_map/ppermute | solution.py:28
  259.1 146.1 %collective-permute-start.26 = (bf16[2,2,64,2048]{3,2,0,1:T(8,128)(2,1)}, bf16[2,2,64,2048]{3,2,0,1:T(8,128)(2,1)}, u32[]{:S(2)}, u32[]{:S(2)}) collective-permute-start(bf16[2,2,64,2048]{3,2,0,1:T(8,128)(2,1)} %dynamic-slice_bitcast_fusion.1), channel_id=1, source_target_pairs={{0,4},{2,6},{4,0},{6,2},{8,12},{10,14},{12,8},{14,10},{16,20},{18,... | collective-permute-start | bytes 3145736 | tf_op jit(solution)/shard_map/ppermute | solution.py:28
  263.3 149.2 %collective-permute-start.30 = (bf16[2,2,64,2048]{3,2,1,0:T(8,128)(2,1)}, bf16[2,2,64,2048]{3,2,1,0:T(8,128)(2,1)}, u32[]{:S(2)}, u32[]{:S(2)}) collective-permute-start(bf16[2,2,64,2048]{3,2,1,0:T(8,128)(2,1)} %dynamic-slice_bitcast_fusion), channel_id=1, source_target_pairs={{0,8},{2,10},{4,12},{6,14},{8,0},{10,2},{12,4},{14,6},{16,24},{18,... | collective-permute-start | bytes 3145736 | tf_op jit(solution)/shard_map/ppermute | solution.py:28
  300.0 56.6 %collective-permute-start.21 = (bf16[2,2,2,64,512]{4,3,2,0,1:T(8,128)(2,1)}, bf16[2,2,2,64,512]{4,3,2,0,1:T(8,128)(2,1)}, u32[]{:S(2)}, u32[]{:S(2)}) collective-permute-start(bf16[2,2,2,64,512]{4,3,2,0,1:T(8,128)(2,1)} %bitcast.262), channel_id=1, source_target_pairs={{0,2},{2,0},{4,6},{6,4},{8,10},{10,8},{12,14},{14,12},{16,18},{18,... | collective-permute-start | bytes 1572872 | tf_op jit(solution)/shard_map/ppermute | solution.py:28
  352.2 15.7 %collective-permute-start.13 = (bf16[2,2,2,64,768]{4,3,0,1,2:T(8,128)(2,1)S(1)}, bf16[2,2,2,64,768]{4,3,0,1,2:T(8,128)(2,1)S(1)}, u32[]{:S(2)}, u32[]{:S(2)}) collective-permute-start(bf16[2,2,2,64,768]{4,3,0,1,2:T(8,128)(2,1)S(1)} %bitcast.293), channel_id=1, source_target_pairs={{0,2},{2,0},{4,6},{6,4},{8,10},{10,8},{12,14},{14,12},{16,18},{18,... | collective-permute-start | bytes 2359304 | tf_op jit(solution)/shard_map/ppermute | solution.py:28
  352.7 17.5 %collective-permute-start.17 = (bf16[2,2,2,64,768]{4,3,2,0,1:T(8,128)(2,1)S(1)}, bf16[2,2,2,64,768]{4,3,2,0,1:T(8,128)(2,1)S(1)}, u32[]{:S(2)}, u32[]{:S(2)}) collective-permute-start(bf16[2,2,2,64,768]{4,3,2,0,1:T(8,128)(2,1)S(1)} %bitcast.292), channel_id=1, source_target_pairs={{0,2},{2,0},{4,6},{6,4},{8,10},{10,8},{12,14},{14,12},{16,18},{18,... | collective-permute-start | bytes 2359304 | tf_op jit(solution)/shard_map/ppermute | solution.py:28
  366.6 24.6 %collective-permute-start.7 = (bf16[512,1024]{1,0:T(8,128)(2,1)S(1)}, bf16[512,1024]{1,0:T(8,128)(2,1)S(1)}, u32[]{:S(2)}, u32[]{:S(2)}) collective-permute-start(bf16[512,1024]{1,0:T(8,128)(2,1)S(1)} %fusion.64), channel_id=1, source_target_pairs={{0,1},{1,0},{2,3},{3,2},{4,5},{5,4},{6,7},{7,6},{8,9},{9,8},{10,11... | collective-permute-start | bytes 3145736 | tf_op jit(solution)/shard_map/ppermute | solution.py:28
  370.2 61.6 %collective-permute-start.14 = (bf16[2,2,64,768]{3,2,0,1:T(8,128)(2,1)}, bf16[2,2,64,768]{3,2,0,1:T(8,128)(2,1)}, u32[]{:S(2)}, u32[]{:S(2)}) collective-permute-start(bf16[2,2,64,768]{3,2,0,1:T(8,128)(2,1)} %dynamic-slice_bitcast_fusion.5), channel_id=1, source_target_pairs={{0,4},{2,6},{4,0},{6,2},{8,12},{10,14},{12,8},{14,10},{16,20},{18,... | collective-permute-start | bytes 1179656 | tf_op jit(solution)/shard_map/ppermute | solution.py:28
  376.3 58.2 %collective-permute-start.18 = (bf16[2,2,64,768]{3,2,1,0:T(8,128)(2,1)}, bf16[2,2,64,768]{3,2,1,0:T(8,128)(2,1)}, u32[]{:S(2)}, u32[]{:S(2)}) collective-permute-start(bf16[2,2,64,768]{3,2,1,0:T(8,128)(2,1)} %dynamic-slice_bitcast_fusion.4), channel_id=1, source_target_pairs={{0,8},{2,10},{4,12},{6,14},{8,0},{10,2},{12,4},{14,6},{16,24},{18,... | collective-permute-start | bytes 1179656 | tf_op jit(solution)/shard_map/ppermute | solution.py:28
  410.1 57.2 %collective-permute-start.27 = (bf16[2,64,2048]{2,1,0:T(8,128)(2,1)}, bf16[2,64,2048]{2,1,0:T(8,128)(2,1)}, u32[]{:S(2)}, u32[]{:S(2)}) collective-permute-start(bf16[2,64,2048]{2,1,0:T(8,128)(2,1)} %dynamic-slice_bitcast_fusion.3), channel_id=1, source_target_pairs={{0,8},{2,10},{4,12},{6,14},{8,0},{10,2},{12,4},{14,6},{16,24},{18,... | collective-permute-start | bytes 1572872 | tf_op jit(solution)/shard_map/ppermute | solution.py:28
  426.1 42.5 %collective-permute-start.31 = (bf16[2,64,2048]{2,1,0:T(8,128)(2,1)S(1)}, bf16[2,64,2048]{2,1,0:T(8,128)(2,1)S(1)}, u32[]{:S(2)}, u32[]{:S(2)}) collective-permute-start(bf16[2,64,2048]{2,1,0:T(8,128)(2,1)S(1)} %dynamic-slice_bitcast_fusion.2), channel_id=1, source_target_pairs={{0,16},{2,18},{4,20},{6,22},{8,24},{10,26},{12,28},{14,30},{16,0},... | collective-permute-start | bytes 1572872 | tf_op jit(solution)/shard_map/ppermute | solution.py:28
  435.8 25.8 %collective-permute-start.19 = (bf16[2,64,768]{2,1,0:T(8,128)(2,1)S(1)}, bf16[2,64,768]{2,1,0:T(8,128)(2,1)S(1)}, u32[]{:S(2)}, u32[]{:S(2)}) collective-permute-start(bf16[2,64,768]{2,1,0:T(8,128)(2,1)S(1)} %dynamic-slice_bitcast_fusion.9), channel_id=1, source_target_pairs={{0,16},{2,18},{4,20},{6,22},{8,24},{10,26},{12,28},{14,30},{16,0},... | collective-permute-start | bytes 589832 | tf_op jit(solution)/shard_map/ppermute | solution.py:28
  444.3 19.4 %collective-permute-start.16 = (bf16[64,768]{1,0:T(8,128)(2,1)S(1)}, bf16[64,768]{1,0:T(8,128)(2,1)S(1)}, u32[]{:S(2)}, u32[]{:S(2)}) collective-permute-start(bf16[64,768]{1,0:T(8,128)(2,1)S(1)} %dynamic-slice_bitcast_fusion.13), channel_id=1, source_target_pairs={{0,16},{2,18},{4,20},{6,22},{8,24},{10,26},{12,28},{14,30},{16,0},... | collective-permute-start | bytes 294920 | tf_op jit(solution)/shard_map/ppermute | solution.py:28
  468.8 14.1 %collective-permute-start.32 = (bf16[64,2048]{1,0:T(8,128)(2,1)S(1)}, bf16[64,2048]{1,0:T(8,128)(2,1)S(1)}, u32[]{:S(2)}, u32[]{:S(2)}) collective-permute-start(bf16[64,2048]{1,0:T(8,128)(2,1)S(1)} %dynamic-slice_bitcast_fusion.6), channel_id=1, source_target_pairs={{0,4},{2,6},{4,0},{6,2},{8,12},{10,14},{12,8},{14,10},{16,20},{18,... | collective-permute-start | bytes 786440 | tf_op jit(solution)/shard_map/ppermute | solution.py:28
  (94 other events, 1123.3 us)
Sparse Core Ops, SparseCore 0:
  10.8 53.2 all-gather.2
  66.8 73.3 all-gather.4
